TPU v7x, 256 devices: a whole 4x4x8 slice. The times are simulated.
256 devices in a mesh: rep: 64 (over y_hi, z, x), fsdp: 4 (over y_lo, core).
Axes of the slice: x: 4, y: 4 (y_hi: 2, y_lo: 2; y = y_hi * 2 + y_lo), z: 8, core: 2. Of those that a mesh axis runs over, the one named last changes fastest.
Arguments:
- inputs: bfloat16 [64, 1024, 4096], P('rep', 'fsdp'), may hold values from -40 to 40
- cotangent: bfloat16 [64, 1024, 512], P('rep', 'fsdp'), may hold values from -6 to 6
- param: float32 [64, 4096, 512], P('rep', 'fsdp'), may hold values from -5 to 5
- momentum: float32 [64, 4096, 512], P('rep', 'fsdp'), may hold values from -3 to 3
- step: int32 [], replicated, may hold values from 0 to 999
Outputs:
- values: bfloat16 [64, 1024, 512], P('rep', 'fsdp')
- input_grad: bfloat16 [64, 1024, 4096], P('rep', 'fsdp')
- new_param: float32 [64, 4096, 512], P('rep', 'fsdp')
- new_momentum: float32 [64, 4096, 512], P('rep', 'fsdp')
All inputs are finite; a program needn't handle non-finite values.
Results may differ from a plain program's by a relative error of at most 0.009.
Values may be sent and summed in bfloat16 or wider, within the bound.
A program may use at most 128 MiB of HBM per device.

v0:
```python
import jax
import jax.numpy as jnp
from jax import lax
from jax.sharding import PartitionSpec as P

EPSILON = 1e-05
MOMENTUM_BETA = 0.9
LEARN_RATE = 0.1
WEIGHT_DECAY = 0.1


def as_sent(x):

    def short(part):
        return part.astype(jnp.bfloat16) if part.dtype == jnp.float32 else part

    return jax.tree.map(short, x)


def from_partner(block, axis, stride):
    count = lax.axis_size(axis)
    route = []
    for low in range(count):
        high = low | 1 << stride
        if high != low and high < count:
            route += [(low, high), (high, low)]
    return lax.ppermute(block, axis, route)


def swap_state(payload, level):

    def branch_for(position):
        return lambda item: jax.tree.map(
            lambda part, own: part.astype(own.dtype),
            from_partner(as_sent(item), "rep", position),
            item,
        )

    count = lax.axis_size("rep").bit_length() - 1
    return lax.switch(level, [branch_for(position) for position in range(count)], payload)


def advance(weights, buffer_in, grad):
    mid_momentum = MOMENTUM_BETA * buffer_in + grad + WEIGHT_DECAY * weights
    mid_param = weights - LEARN_RATE * mid_momentum
    return (mid_param, mid_momentum)


def on_device(inputs, cotangent, param, momentum, step):
    width = inputs.shape[2]
    scale = width ** (-0.5)
    levels = lax.axis_size("rep").bit_length() - 1
    level = jnp.remainder(step, levels)
    weights = param[0]
    buffer_in = momentum[0]
    upstream = cotangent[0]
    floats = inputs[0].astype(jnp.float32)
    inverse_rms = lax.rsqrt(jnp.mean(floats * floats, axis=-1, keepdims=True) + EPSILON)
    normed = (floats * inverse_rms).astype(jnp.bfloat16)
    weights_half = weights.astype(jnp.bfloat16)
    piece = lax.all_gather(weights_half, "fsdp", axis=0, tiled=True)
    columns = normed
    forward_sum = jnp.dot(columns, piece, preferred_element_type=jnp.float32)
    back_part = lax.dot_general(
        upstream, piece, (((1,), (1,)), ((), ())), preferred_element_type=jnp.float32
    )
    normed_grad = back_part
    forward_sum, normed_grad = (forward_sum, normed_grad)
    values = (scale * forward_sum).astype(jnp.bfloat16)
    normed_grad = scale * normed_grad
    projection = jnp.sum(normed_grad * floats, axis=-1, keepdims=True) / width
    input_grad = (inverse_rms * normed_grad - inverse_rms**3 * floats * projection).astype(
        jnp.bfloat16
    )
    columns = normed
    grad = lax.psum_scatter(
        (
            scale
            * lax.dot_general(
                columns, upstream, (((0,), (0,)), ((), ())), preferred_element_type=jnp.float32
            )
        ).astype(jnp.bfloat16),
        "fsdp",
        scatter_dimension=0,
        tiled=True,
    ).astype(jnp.float32)
    mid_param, mid_momentum = advance(weights, buffer_in, grad)
    other_param, other_momentum = swap_state((mid_param, mid_momentum), level)
    new_param = 0.5 * (mid_param + other_param)
    new_momentum = 0.5 * (mid_momentum + other_momentum)
    return (values[None], input_grad[None], new_param[None], new_momentum[None])


def solution(mesh):
    placed = (
        P("rep", "fsdp", None),
        P("rep", "fsdp", None),
        P("rep", "fsdp", None),
        P("rep", "fsdp", None),
        P(),
    )
    return jax.shard_map(
        on_device,
        mesh=mesh,
        in_specs=placed,
        out_specs=(
            P("rep", "fsdp", None),
            P("rep", "fsdp", None),
            P("rep", "fsdp", None),
            P("rep", "fsdp", None),
        ),
        check_vma=False,
    )
```

profile of v0, /device:TPU:1, one launch (start us, length us, event | category | flops | bytes accessed | tf_op | source)
XLA Modules:
  0.0 190.5 jit_solution(4506977374094245174)
XLA Ops:
  7.2 0.0 copy-start
  7.2 0.0 copy-start.2
  7.2 0.0 all-gather.2.cloned.1.call-start
  7.2 2.8 %bitcast_convert_fusion = bf16[1024,512]{1,0:T(8,128)(2,1)} fusion(f32[1,1024,512]{2,1,0:T(8,128)} %param.13), kind=kLoop, calls=%fused_computation.21 | loop fusion | flops 524288 | bytes 3145728 | tf_op jit(solution)/shard_map/convert_element_type | solution.py:60
  10.1 0.0 all-gather.2.cloned.1.call-update
  10.1 0.0 reduce-scatter.2.cloned.1.call-start
  10.2 53.6 %all-gather.2.cloned.1.call-done = bf16[4096,512]{1,0:T(8,128)(2,1)} async-done(((bf16[1024,512]{1,0:T(8,128)(2,1)}), bf16[4096,512]{1,0:T(8,128)(2,1)}) %all-gather.2.cloned.1.call-update) | async-done | bytes 4194320 | tf_op jit(solution)/shard_map/all_gather | solution.py:61
  63.8 0.0 copy-done
  63.8 0.0 copy-done.2
  63.8 5.5 %fusion.9 = (f32[256]{0:T(256)S(1)}, f32[256]{0:T(256)S(1)}, f32[256,4096]{1,0:T(8,128)}) fusion(bf16[1,256,4096]{2,1,0:T(8,128)(2,1)S(1)} %copy-done.2, bf16[4096,512]{1,0:T(8,128)(2,1)} %all-gather.2.cloned.1.call-done, bf16[1,256,512]{2,1,0:T(8,128)(2,1)S(1)} %copy-done), kind=kOutput, calls=%fused_computation.12 | convolution fusion | flops 1080032768 | bytes 10749952 | tf_op jit(solution)/shard_map/dot_general | solution.py:64
  69.2 3.4 %multiply_convert_fusion = bf16[4096,512]{1,0:T(8,128)(2,1)} fusion(bf16[1,256,4096]{2,1,0:T(8,128)(2,1)S(1)} %copy-done.2, f32[256]{0:T(256)S(1)} %get-tuple-element.68, bf16[1,256,512]{2,1,0:T(8,128)(2,1)S(1)} %copy-done), kind=kOutput, calls=%fused_computation | convolution fusion | flops 1081081856 | bytes 6554624 | tf_op jit(solution)/shard_map/dot_general | solution.py:79
  72.6 0.0 reduce-scatter.2.cloned.1.call-update
  73.3 0.0 copy-start.1
  73.3 4.3 %fusion.25 = bf16[1,256,512]{2,1,0:T(8,128)(2,1)} fusion(bf16[4096,512]{1,0:T(8,128)(2,1)} %all-gather.2.cloned.1.call-done, bf16[1,256,4096]{2,1,0:T(8,128)(2,1)S(1)} %copy-done.2, f32[256]{0:T(256)S(1)} %get-tuple-element.68), kind=kOutput, calls=%fused_computation.28 | convolution fusion | flops 1077149696 | bytes 6554624 | tf_op jit(solution)/shard_map/dot_general | solution.py:63
  77.7 0.0 copy-done.1
  77.7 2.6 %fusion.13 = bf16[1,256,4096]{2,1,0:T(8,128)(2,1)} fusion(bf16[1,256,4096]{2,1,0:T(8,128)(2,1)S(1)} %copy-done.2, f32[256,4096]{1,0:T(8,128)S(1)} %copy-done.1, f32[256]{0:T(256)S(1)} %broadcast_multiply_fusion.1, f32[256]{0:T(256)S(1)} %get-tuple-element.67, f32[256]{0:T(256)S(1)} %get-tuple-element.66), kind=kLoop, calls=%fused_computation.15 | loop fusion | flops 6291456 | bytes 8391680 | tf_op jit(solution)/shard_map/broadcast_in_dim | solution.py:91
  80.3 41.2 %reduce-scatter.2.cloned.1.call-done = bf16[1024,512]{1,0:T(8,128)(2,1)} async-done(((bf16[4096,512]{1,0:T(8,128)(2,1)}), bf16[1024,512]{1,0:T(8,128)(2,1)}) %reduce-scatter.2.cloned.1.call-update) | async-done | bytes 1048592 | tf_op jit(solution)/shard_map/reduce_scatter | solution.py:76
  121.5 4.6 %bitcast_subtract_fusion = (f32[1024,512]{1,0:T(8,128)S(1)}, f32[1024,512]{1,0:T(8,128)}) fusion(f32[1,1024,512]{2,1,0:T(8,128)} %param.13, bf16[1024,512]{1,0:T(8,128)(2,1)} %reduce-scatter.2.cloned.1.call-done, f32[1,1024,512]{2,1,0:T(8,128)} %param.14), kind=kLoop, calls=%fused_computation.19 | loop fusion | flops 3670016 | bytes 9437184 | tf_op jit(solution)/shard_map/sub | solution.py:45
  126.0 51.7 %conditional.4 = (f32[1024,512]{1,0:T(8,128)}, f32[1024,512]{1,0:T(8,128)}) conditional(s32[]{:T(128)} %clamp.3, (f32[1024,512]{1,0:T(8,128)S(1)}, f32[1024,512]{1,0:T(8,128)}) %bitcast_subtract_fusion, (f32[1024,512]{1,0:T(8,128)S(1)}, f32[1024,512]{1,0:T(8,128)}) %bitcast_subtract_fusion, ...), branch_computations={%region_3.4_spmd, %region_4.5_spmd, %region_5.6_spmd, %region_6.7_... | conditional | flops 2097152 | bytes 20971616
  126.0 1.7 convert_element_type.119
  127.8 2.5 %collective-permute-start.11 = (bf16[1024,512]{1,0:T(8,128)(2,1)S(1)}, bf16[1024,512]{1,0:T(8,128)(2,1)S(1)}, u32[]{:S(2)}, u32[]{:S(2)}) collective-permute-start(bf16[1024,512]{1,0:T(8,128)(2,1)S(1)} %convert_element_type.119), channel_id=1, source_target_pairs={{0,128},{128,0},{4,132},{132,4},{8,136},{136,8},{12,140},{140,12},... | collective-permute-start | bytes 3145736 | tf_op jit(solution)/shard_map/cond/branch_5_fun/ppermute | solution.py:27
  130.3 0.1 convert_element_type.117
  130.4 0.6 collective-permute-start.10
  131.0 22.7 %collective-permute-done.11 = bf16[1024,512]{1,0:T(8,128)(2,1)S(1)} collective-permute-done((bf16[1024,512]{1,0:T(8,128)(2,1)S(1)}, bf16[1024,512]{1,0:T(8,128)(2,1)S(1)}, u32[]{:S(2)}, u32[]{:S(2)}) %collective-permute-start.11) | collective-permute-done | bytes 1048608 | tf_op jit(solution)/shard_map/cond/branch_5_fun/ppermute | solution.py:27
  153.7 1.6 convert_element_type.157
  155.3 20.8 %collective-permute-done.10 = bf16[1024,512]{1,0:T(8,128)(2,1)S(1)} collective-permute-done((bf16[1024,512]{1,0:T(8,128)(2,1)S(1)}, bf16[1024,512]{1,0:T(8,128)(2,1)S(1)}, u32[]{:S(2)}, u32[]{:S(2)}) %collective-permute-start.10) | collective-permute-done | bytes 1048608 | tf_op jit(solution)/shard_map/cond/branch_5_fun/ppermute | solution.py:27
  176.2 1.6 convert_element_type.151
  177.8 5.9 %multiply_bitcast_fusion = (f32[1,1024,512]{2,1,0:T(8,128)}, f32[1,1024,512]{2,1,0:T(8,128)}) fusion(f32[1024,512]{1,0:T(8,128)} %get-tuple-element.65, f32[1024,512]{1,0:T(8,128)} %get-tuple-element.61, f32[1024,512]{1,0:T(8,128)S(1)} %get-tuple-element.64, f32[1024,512]{1,0:T(8,128)} %get-tuple-element.60), kind=kLoop, calls=%fused_computation.22 | loop fusion | flops 2097152 | bytes 12582912 | tf_op jit(solution)/shard_map/broadcast_in_dim | solution.py:91
  (2 shorter events, 0.0 us)
Async XLA Ops:
  7.2 56.6 %copy-start = (bf16[1,256,512]{2,1,0:T(8,128)(2,1)S(1)}, bf16[1,256,512]{2,1,0:T(8,128)(2,1)}, u32[]{:S(2)}) copy-start(bf16[1,256,512]{2,1,0:T(8,128)(2,1)} %param.12) | copy-start | bytes 786436
  7.2 56.6 %copy-start.2 = (bf16[1,256,4096]{2,1,0:T(8,128)(2,1)S(1)}, bf16[1,256,4096]{2,1,0:T(8,128)(2,1)}, u32[]{:S(2)}) copy-start(bf16[1,256,4096]{2,1,0:T(8,128)(2,1)} %param.11) | copy-start | bytes 6291460
  7.2 56.6 %all-gather.2.cloned.1.call-start = ((), (), s32[]{:S(2)}) async-start(), calls=%async_computation.1 | async-start | bytes 5242880 | tf_op jit(solution)/shard_map/all_gather | solution.py:61
  10.1 111.4 %reduce-scatter.2.cloned.1.call-start = ((), (), s32[]{:S(2)}) async-start(), calls=%async_computation.2 | async-start | bytes 5242880 | tf_op jit(solution)/shard_map/reduce_scatter | solution.py:76
  73.3 4.3 %copy-start.1 = (f32[256,4096]{1,0:T(8,128)S(1)}, f32[256,4096]{1,0:T(8,128)}, u32[]{:S(2)}) copy-start(f32[256,4096]{1,0:T(8,128)} %get-tuple-element.69) | copy-start | bytes 12582916
  127.8 25.9 %collective-permute-start.11 = (bf16[1024,512]{1,0:T(8,128)(2,1)S(1)}, bf16[1024,512]{1,0:T(8,128)(2,1)S(1)}, u32[]{:S(2)}, u32[]{:S(2)}) collective-permute-start(bf16[1024,512]{1,0:T(8,128)(2,1)S(1)} %convert_element_type.119), channel_id=1, source_target_pairs={{0,128},{128,0},{4,132},{132,4},{8,136},{136,8},{12,140},{140,12},... | collective-permute-start | bytes 3145736 | tf_op jit(solution)/shard_map/cond/branch_5_fun/ppermute | solution.py:27
  130.4 45.7 %collective-permute-start.10 = (bf16[1024,512]{1,0:T(8,128)(2,1)S(1)}, bf16[1024,512]{1,0:T(8,128)(2,1)S(1)}, u32[]{:S(2)}, u32[]{:S(2)}) collective-permute-start(bf16[1024,512]{1,0:T(8,128)(2,1)S(1)} %convert_element_type.117), channel_id=1, source_target_pairs={{0,128},{128,0},{4,132},{132,4},{8,136},{136,8},{12,140},{140,12},... | collective-permute-start | bytes 3145736 | tf_op jit(solution)/shard_map/cond/branch_5_fun/ppermute | solution.py:27
Sparse Core Ops, SparseCore 0:
  10.4 53.3 all-gather.1
  72.8 48.6 reduce-scatter.1
where the time goes:
time: 191 us
  waiting for transfers between devices  138 us (72%)
  other arithmetic  21 us (11%)
  between operations  14.7 us (8%)
  matrix products  13.2 us (7%)
  starting transfers between devices  3.22 us (2%)
    all_gather x1, waiting for transfers between devices, on_device(): piece = lax.all_gather(weights_half, 'fsdp', axis=0, tiled=True)  53.6 us
    ppermute x2, waiting for transfers between devices, from_partner(): return lax.ppermute(block, axis, route)  43.5 us
    reduce_scatter x1, waiting for transfers between devices, on_device(): lax.psum_scatter((scale * lax.dot_general(columns, upstream, (((0,), (0,)...  41.2 us
    broadcast_in_dim x2, other arithmetic, on_device(): return (values[None], input_grad[None], new_param[None], new_momentum[None])  8.5 us
    dot_general x1, matrix products, on_device(): lax.dot_general(upstream, piece, (((1,), (1,)), ((), ())), preferred_elem...  5.47 us
    sub x1, other arithmetic, advance(): mid_param = weights - LEARN_RATE * mid_momentum  4.56 us
    dot_general x1, matrix products, on_device(): forward_sum = jnp.dot(columns, piece, preferred_element_type=jnp.float32)  4.33 us
  transfers between devices with their start and end apart: 4, of which 4 were waited for; matrix products, arithmetic and copies ran while one was open for 5% of the time, Pallas kernels for 0%

commit v1 on v0

v1 whole, which is shorter than its diff:
```python
import functools

import jax
import jax.numpy as jnp
from jax import lax
from jax.experimental import pallas as pl
from jax.experimental.pallas import tpu as pltpu
from jax.sharding import PartitionSpec as P

EPSILON = 1e-05
MOMENTUM_BETA = 0.9
LEARN_RATE = 0.1
WEIGHT_DECAY = 0.1

MESH = pl.DeviceIdType.MESH
F32 = jnp.float32
BF16 = jnp.bfloat16

CHUNK = 128
EARLY = 2


def dot(a, b, ca, cb):
    return lax.dot_general(a, b, (((ca,), (cb,)), ((), ())), preferred_element_type=F32)


def kernel(
    stride,
    x_hbm, c_hbm, p_hbm, m_hbm,
    val_hbm, ig_hbm, np_hbm, nm_hbm,
    xv, xs, cv, cs, css, pv, mv, w, gs, gr, rp, ms, rm, fwd, back, inv, vv, igv,
    in_p, in_x, in_c, in_m, out_v, out_ig, out_p, out_m,
    xs_s, xs_r, cs_s, cs_r, ya_s, ya_r, so_s, so_r, sf_s, sf_r,
    g_s, g_r, ep_s, ep_r, em_s, em_r,
):
    tokens, width = xv.shape
    rows, units = pv.shape
    scale = width ** (-0.5)
    n = rows // CHUNK

    rep = lax.axis_index("rep")
    f = lax.axis_index("fsdp")
    f1 = f + 1 - 2 * lax.rem(f, 2)
    f2 = f + 2 - 4 * lax.div(f, 2)
    f3 = f1 + 2 - 4 * lax.div(f, 2)
    partner = rep + stride * (1 - 2 * lax.rem(lax.div(rep, stride), 2))
    sib, across, peer = (rep, f1), (rep, f2), (partner, f)

    def part(k):
        return pl.ds(pl.multiple_of(k * CHUNK, CHUNK), CHUNK)

    def cols(owner, k):
        return pl.ds(pl.multiple_of(owner * rows + k * CHUNK, CHUNK), CHUNK)

    def block(owner):
        return pl.ds(pl.multiple_of(owner * rows, rows), rows)

    def remote(src, dst, send, recv, where):
        return pltpu.make_async_remote_copy(
            src_ref=src, dst_ref=dst, send_sem=send, recv_sem=recv,
            device_id=where, device_id_type=MESH,
        )

    def load_p(k):
        return pltpu.make_async_copy(p_hbm.at[part(k)], pv.at[part(k)], in_p.at[k])

    load_x = pltpu.make_async_copy(x_hbm, xv, in_x)
    load_c = pltpu.make_async_copy(c_hbm, cv, in_c)
    load_m = pltpu.make_async_copy(m_hbm, mv, in_m)

    def send_x(j, owner):
        return remote(x_hbm.at[:, block(owner)], xs.at[j], xs_s.at[j], xs_r.at[j], sib)

    send_c = remote(cs, css, cs_s, cs_r, sib)

    def gather_y(k):
        ref = w.at[f, part(k)]
        return remote(ref, ref, ya_s.at[k], ya_r.at[k], across)

    def gather_own(k):
        ref = w.at[f, part(k)]
        return remote(ref, ref, so_s.at[k], so_r.at[k], sib)

    def gather_fwd(k):
        ref = w.at[f2, part(k)]
        return remote(ref, ref, sf_s.at[k], sf_r.at[k], sib)

    def send_g(k):
        return remote(gs.at[part(k)], gr.at[part(k)], g_s.at[k], g_r.at[k], across)

    def swap_p(k):
        return remote(w.at[f, part(k)], rp.at[part(k)], ep_s.at[k], ep_r.at[k], peer)

    def swap_m(k):
        return remote(ms.at[part(k)], rm.at[part(k)], em_s.at[k], em_r.at[k], peer)

    def store_p(k):
        return pltpu.make_async_copy(pv.at[part(k)], np_hbm.at[part(k)], out_p.at[k])

    def store_m(k):
        return pltpu.make_async_copy(mv.at[part(k)], nm_hbm.at[part(k)], out_m.at[k])

    def loop(low, high, body):
        def step(k, carry):
            body(k)
            return carry
        lax.fori_loop(low, high, step, 0)

    barrier = pltpu.get_barrier_semaphore()
    for where in (sib, across, peer):
        pl.semaphore_signal(barrier, inc=1, device_id=where, device_id_type=MESH)
    loop(0, n, lambda k: load_p(k).start())
    load_x.start()
    load_c.start()
    load_m.start()
    pl.semaphore_wait(barrier, 3)

    def begin(k):
        load_p(k).wait()
        w[f, part(k)] = pv[part(k)].astype(BF16)
        swap_p(k).start()

        @pl.when(k < EARLY)
        def _():
            gather_y(k).start()

    loop(0, EARLY, begin)
    send_x(1, f3).start()
    send_x(0, f1).start()
    loop(EARLY, n, begin)
    loop(0, n, lambda k: gather_own(k).start())

    load_x.wait()
    load_c.wait()

    def square(j, total):
        part_x = xv[:, pl.ds(pl.multiple_of(j * 512, 512), 512)].astype(F32)
        return total + jnp.sum(part_x * part_x, axis=1, keepdims=True)

    total = lax.fori_loop(0, width // 512, square, jnp.zeros((tokens, 1), F32))
    inverse = lax.rsqrt(total / width + EPSILON)
    inv[...] = inverse
    cs[...] = (inverse * cv[...].astype(F32)).astype(BF16)
    send_c.start()

    def term(owner, j, k):
        mine = dot(xv[:, cols(owner, k)], cs[...], 0, 0)
        theirs = dot(xs[j, :, part(k)], css[...], 0, 0)
        return scale * (mine + theirs)

    send_x(1, f3).wait_recv()
    send_c.wait_recv()

    def give(k):
        gs[part(k)] = term(f2, 1, k).astype(BF16)
        send_g(k).start()

    loop(0, n, give)

    send_x(0, f1).wait_recv()
    load_m.wait()

    def keep(k):
        at = part(k)
        mv[at] = MOMENTUM_BETA * mv[at] + WEIGHT_DECAY * pv[at] + term(f, 0, k)

    loop(0, n, keep)

    def product(owner, k):
        piece = w[owner, part(k)]
        fwd[...] += dot(xv[:, cols(owner, k)], piece, 1, 0)
        back[:, cols(owner, k)] = dot(cv[...], piece, 1, 1)

    fwd[...] = jnp.zeros_like(fwd)

    def near(k):
        product(f, k)
        gather_own(k).wait_recv()
        product(f1, k)

    def pass_on(k):
        gather_y(k).wait_recv()
        gather_fwd(k).start()

    def far(k):
        product(f2, k)
        gather_fwd(k).wait_recv()
        product(f3, k)

    loop(0, EARLY, pass_on)
    loop(0, n, near)
    loop(0, EARLY, far)

    def fold(k):
        at = part(k)
        send_g(k).wait_recv()
        mid = mv[at] + gr[at].astype(F32)
        mv[at] = mid
        ms[at] = mid.astype(BF16)
        swap_m(k).start()

    def mix(k):
        at = part(k)
        swap_p(k).wait_recv()
        swap_m(k).wait_recv()
        momentum = 0.5 * (mv[at] + rm[at].astype(F32))
        mv[at] = momentum
        store_m(k).start()
        pv[at] = 0.5 * (pv[at] + rp[at].astype(F32)) - LEARN_RATE * momentum
        store_p(k).start()

    loop(0, n - 1, fold)
    loop(EARLY, n, lambda k: gather_y(k).start())
    fold(n - 1)

    def rest(k):
        pass_on(k)
        mix(k - EARLY)
        far(k)

    loop(EARLY, n, rest)

    inverse = inv[...]
    vv[...] = (scale * inverse * fwd[...]).astype(BF16)
    store_v = pltpu.make_async_copy(vv, val_hbm, out_v)
    store_v.start()
    projection = scale * jnp.sum(fwd[...] * cv[...].astype(F32), axis=1, keepdims=True) / width
    first = scale * inverse
    second = inverse**3 * projection

    def store_ig(j):
        at = pl.ds(pl.multiple_of(j * 512, 512), 512)
        return pltpu.make_async_copy(igv.at[:, at], ig_hbm.at[:, at], out_ig.at[j])

    def finish(j):
        at = pl.ds(pl.multiple_of(j * 512, 512), 512)
        igv[:, at] = (first * back[:, at] - second * xv[:, at].astype(F32)).astype(BF16)
        store_ig(j).start()

    loop(0, width // 512, finish)
    loop(n - EARLY, n, mix)

    store_v.wait()
    loop(0, width // 512, lambda j: store_ig(j).wait())
    send_x(0, f1).wait_send()
    send_x(1, f3).wait_send()
    send_c.wait_send()

    def drain(k):
        store_p(k).wait()
        store_m(k).wait()
        gather_y(k).wait_send()
        gather_own(k).wait_send()
        gather_fwd(k).wait_send()
        send_g(k).wait_send()
        swap_p(k).wait_send()
        swap_m(k).wait_send()

    loop(0, n, drain)


def run(level, x, c, p, m):
    tokens, width = x.shape
    rows, units = p.shape
    n = rows // CHUNK
    dma = pltpu.SemaphoreType.DMA
    anywhere = pl.BlockSpec(memory_space=pl.ANY)
    vmem = pltpu.VMEM
    return pl.pallas_call(
        functools.partial(kernel, 2**level),
        out_shape=(
            jax.ShapeDtypeStruct((tokens, units), BF16),
            jax.ShapeDtypeStruct((tokens, width), BF16),
            jax.ShapeDtypeStruct((rows, units), F32),
            jax.ShapeDtypeStruct((rows, units), F32),
        ),
        in_specs=[anywhere] * 4,
        out_specs=(anywhere,) * 4,
        scratch_shapes=[
            vmem((tokens, width), BF16),
            vmem((2, tokens, rows), BF16),
            vmem((tokens, units), BF16),
            vmem((tokens, units), BF16),
            vmem((tokens, units), BF16),
            vmem((rows, units), F32),
            vmem((rows, units), F32),
            vmem((4, rows, units), BF16),
            vmem((rows, units), BF16),
            vmem((rows, units), BF16),
            vmem((rows, units), BF16),
            vmem((rows, units), BF16),
            vmem((rows, units), BF16),
            vmem((tokens, units), F32),
            vmem((tokens, width), F32),
            vmem((tokens, 1), F32),
            vmem((tokens, units), BF16),
            vmem((tokens, width), BF16),
            dma((n,)), dma, dma, dma, dma, dma((width // 512,)), dma((n,)), dma((n,)),
            dma((2,)), dma((2,)), dma, dma,
            dma((n,)), dma((n,)), dma((n,)), dma((n,)), dma((n,)), dma((n,)),
            dma((n,)), dma((n,)), dma((n,)), dma((n,)), dma((n,)), dma((n,)),
        ],
        compiler_params=pltpu.CompilerParams(
            collective_id=level, has_side_effects=True, vmem_limit_bytes=48 * 2**20
        ),
        name="window" + str(level),
    )(x, c, p, m)


def on_device(inputs, cotangent, param, momentum, step):
    levels = lax.axis_size("rep").bit_length() - 1
    level = jnp.remainder(step, levels)
    outs = lax.switch(
        level,
        [functools.partial(run, position) for position in range(levels)],
        inputs[0], cotangent[0], param[0], momentum[0],
    )
    return tuple(out[None] for out in outs)


def solution(mesh):
    placed = P("rep", "fsdp", None)
    return jax.shard_map(
        on_device,
        mesh=mesh,
        in_specs=(placed, placed, placed, placed, P()),
        out_specs=(placed,) * 4,
        check_vma=False,
    )
```

time: 191 us -> 61.2 us (0.32)
  waiting for transfers between devices: 138 us -> 0 us
  Pallas kernels: 0 us -> 54.9 us
  other arithmetic: 21 us -> 0 us
  between operations: 14.7 us -> 1.3 us
  matrix products: 13.2 us -> 0 us
  local copies, waits for them, and re-layouts: 0.02 us -> 4.66 us
  starting transfers between devices: 3.22 us -> 0 us
    pallas_call x0 -> x1, Pallas kernels: none -> 54.9 us  [run(): pl.pallas_call(functools.partial(kernel, 2 ** level), out_shape=(jax.Shap...]
    all_gather x1 -> x0, waiting for transfers between devices: 53.6 us -> none  [on_device(): piece = lax.all_gather(weights_half, 'fsdp', axis=0, tiled=True)]
    ppermute x2 -> x0, waiting for transfers between devices: 43.5 us -> none  [from_partner(): return lax.ppermute(block, axis, route)]
    reduce_scatter x1 -> x0, waiting for transfers between devices: 41.2 us -> none  [on_device(): lax.psum_scatter((scale * lax.dot_general(columns, upstream, (((0,), (0,)...]
    dot_general x3 -> x0, matrix products: 13.2 us -> none  [the longest x1 5.47 us: on_device(): lax.dot_general(upstream, piece, (((1,), (1,)), ((), ())), preferred_elem...]
    broadcast_in_dim x2 -> x0, other arithmetic: 8.5 us -> none  [on_device(): return (values[None], input_grad[None], new_param[None], new_momentum[None])]
    convert_element_type x5 -> x0, other arithmetic: 7.94 us -> none  [the longest x2 3.24 us: branch_for(): part.astype(own.dtype)]
    unnamed x6 -> x4, local copies, waits for them, and re-layouts: 0.02 us -> 4.66 us
  transfers between devices with their start and end apart: 4 -> 0, of which waited for: 4 -> 0; matrix products, arithmetic and copies ran while one was open for 5% -> 0% of each run, Pallas kernels for 0% -> 0%
where the time goes in v1:
time: 61.2 us; the launch traced here: 61.1 us
  Pallas kernels  54.9 us (90%)
  local copies, waits for them, and re-layouts  4.66 us (8%)
  between operations  1.3 us (2%)
    pallas_call x1, Pallas kernels, run(): pl.pallas_call(functools.partial(kernel, 2 ** level), out_shape=(jax.Shap...  54.9 us
    unnamed x4, local copies, waits for them, and re-layouts  4.66 us

profile of v1, /device:TPU:1, one launch (start us, length us, event | category | flops | bytes accessed | tf_op | source)
XLA Modules:
  0.0 61.1 jit_solution(7758216308903629021)
XLA Ops:
  1.3 55.2 %conditional.1 = ((bf16[256,512]{1,0:T(8,128)(2,1)S(1)}, bf16[256,4096]{1,0:T(8,128)(2,1)S(1)}, f32[1024,512]{1,0:T(8,128)S(1)}, f32[1024,512]{1,0:T(8,128)S(1)})) conditional(s32[]{:T(128)} %clamp.3, (bf16[256,4096]{1,0:T(8,128)(2,1)}, bf16[256,512]{1,0:T(8,128)(2,1)}, f32[1024,512]{1,0:T(8,128)}, ...), branch_computations={%region_0.1_spmd, %region_1.2_spmd, %region_2.3_spmd, %region_3.4_... | conditional | bytes 8 | solution.py:313
  1.3 54.9 %window2.1 = (bf16[256,512]{1,0:T(8,128)(2,1)S(1)}, bf16[256,4096]{1,0:T(8,128)(2,1)S(1)}, f32[1024,512]{1,0:T(8,128)S(1)}, f32[1024,512]{1,0:T(8,128)S(1)}) custom-call(bf16[256,4096]{1,0:T(8,128)(2,1)} %get-tuple-element.92.x_hbm, bf16[256,512]{1,0:T(8,128)(2,1)} %get-tuple-element.93.c_hbm, f32[1024,512]{1,0:T(8,128)} %get-tuple-element.94.p_hbm, ...), custom_call_target="tpu_custom_call" | custom-call | tf_op jit(solution)/shard_map/cond/branch_2_fun/window2/pallas_call | solution.py:269
  56.5 0.7 %copy.38 = bf16[1,256,512]{2,1,0:T(8,128)(2,1)} copy(bf16[1,256,512]{2,1,0:T(8,128)(2,1)S(1)} %bitcast.35) | data formatting | bytes 524288
  57.2 1.3 %copy.39 = bf16[1,256,4096]{2,1,0:T(8,128)(2,1)} copy(bf16[1,256,4096]{2,1,0:T(8,128)(2,1)S(1)} %bitcast.32) | data formatting | bytes 4194304
  58.5 1.3 %copy.40 = f32[1,1024,512]{2,1,0:T(8,128)} copy(f32[1,1024,512]{2,1,0:T(8,128)S(1)} %bitcast.33) | data formatting | bytes 4194304
  59.8 1.3 %copy.41 = f32[1,1024,512]{2,1,0:T(8,128)} copy(f32[1,1024,512]{2,1,0:T(8,128)S(1)} %bitcast.34) | data formatting | bytes 4194304

commit v2 on v1

--- a/solution.py
+++ b/solution.py
@@ -17,7 +17,7 @@
 BF16 = jnp.bfloat16
 
 CHUNK = 128
-EARLY = 2
+PIECES = 4
 
 
 def dot(a, b, ca, cb):
@@ -25,11 +25,11 @@
 
 
 def kernel(
-    stride,
+    stride, early, relay,
     x_hbm, c_hbm, p_hbm, m_hbm,
-    val_hbm, ig_hbm, np_hbm, nm_hbm,
-    xv, xs, cv, cs, css, pv, mv, w, gs, gr, rp, ms, rm, fwd, back, inv, vv, igv,
-    in_p, in_x, in_c, in_m, out_v, out_ig, out_p, out_m,
+    vv, xv, back, factors, pv, rp, mv, rm,
+    xs, cv, cs, css, w, gs, gr, ms, fwd, inv,
+    in_p, in_x, in_c, in_m,
     xs_s, xs_r, cs_s, cs_r, ya_s, ya_r, so_s, so_r, sf_s, sf_r,
     g_s, g_r, ep_s, ep_r, em_s, em_r,
 ):
@@ -44,7 +44,7 @@
     f2 = f + 2 - 4 * lax.div(f, 2)
     f3 = f1 + 2 - 4 * lax.div(f, 2)
     partner = rep + stride * (1 - 2 * lax.rem(lax.div(rep, stride), 2))
-    sib, across, peer = (rep, f1), (rep, f2), (partner, f)
+    sib, across, peer, beyond = (rep, f1), (rep, f2), (partner, f), (partner, f2)
 
     def part(k):
         return pl.ds(pl.multiple_of(k * CHUNK, CHUNK), CHUNK)
@@ -86,19 +86,15 @@
         return remote(ref, ref, sf_s.at[k], sf_r.at[k], sib)
 
     def send_g(k):
-        return remote(gs.at[part(k)], gr.at[part(k)], g_s.at[k], g_r.at[k], across)
+        where = (rep + lax.rem(k, 2) * (partner - rep), f2) if relay else across
+        return remote(gs.at[part(k)], gr.at[part(k)], g_s.at[k], g_r.at[k], where)
 
     def swap_p(k):
-        return remote(w.at[f, part(k)], rp.at[part(k)], ep_s.at[k], ep_r.at[k], peer)
+        owner, where = (f2, beyond) if relay else (f, peer)
+        return remote(w.at[owner, part(k)], rp.at[part(k)], ep_s.at[k], ep_r.at[k], where)
 
     def swap_m(k):
         return remote(ms.at[part(k)], rm.at[part(k)], em_s.at[k], em_r.at[k], peer)
-
-    def store_p(k):
-        return pltpu.make_async_copy(pv.at[part(k)], np_hbm.at[part(k)], out_p.at[k])
-
-    def store_m(k):
-        return pltpu.make_async_copy(mv.at[part(k)], nm_hbm.at[part(k)], out_m.at[k])
 
     def loop(low, high, body):
         def step(k, carry):
@@ -107,27 +103,29 @@
         lax.fori_loop(low, high, step, 0)
 
     barrier = pltpu.get_barrier_semaphore()
-    for where in (sib, across, peer):
+    friends = (sib, across, peer, beyond) if relay else (sib, across, peer)
+    for where in friends:
         pl.semaphore_signal(barrier, inc=1, device_id=where, device_id_type=MESH)
     loop(0, n, lambda k: load_p(k).start())
     load_x.start()
     load_c.start()
     load_m.start()
-    pl.semaphore_wait(barrier, 3)
+    pl.semaphore_wait(barrier, len(friends))
 
     def begin(k):
         load_p(k).wait()
         w[f, part(k)] = pv[part(k)].astype(BF16)
-        swap_p(k).start()
-
-        @pl.when(k < EARLY)
+        if not relay:
+            swap_p(k).start()
+
+        @pl.when(k < early)
         def _():
             gather_y(k).start()
 
-    loop(0, EARLY, begin)
+    loop(0, early, begin)
     send_x(1, f3).start()
     send_x(0, f1).start()
-    loop(EARLY, n, begin)
+    loop(early, n, begin)
     loop(0, n, lambda k: gather_own(k).start())
 
     load_x.wait()
@@ -181,15 +179,17 @@
     def pass_on(k):
         gather_y(k).wait_recv()
         gather_fwd(k).start()
+        if relay:
+            swap_p(k).start()
 
     def far(k):
         product(f2, k)
         gather_fwd(k).wait_recv()
         product(f3, k)
 
-    loop(0, EARLY, pass_on)
+    loop(0, early, pass_on)
     loop(0, n, near)
-    loop(0, EARLY, far)
+    loop(0, early, far)
 
     def fold(k):
         at = part(k)
@@ -199,56 +199,29 @@
         ms[at] = mid.astype(BF16)
         swap_m(k).start()
 
-    def mix(k):
-        at = part(k)
-        swap_p(k).wait_recv()
-        swap_m(k).wait_recv()
-        momentum = 0.5 * (mv[at] + rm[at].astype(F32))
-        mv[at] = momentum
-        store_m(k).start()
-        pv[at] = 0.5 * (pv[at] + rp[at].astype(F32)) - LEARN_RATE * momentum
-        store_p(k).start()
-
     loop(0, n - 1, fold)
-    loop(EARLY, n, lambda k: gather_y(k).start())
+    loop(early, n, lambda k: gather_y(k).start())
     fold(n - 1)
 
     def rest(k):
         pass_on(k)
-        mix(k - EARLY)
         far(k)
 
-    loop(EARLY, n, rest)
+    loop(early, n, rest)
 
     inverse = inv[...]
     vv[...] = (scale * inverse * fwd[...]).astype(BF16)
-    store_v = pltpu.make_async_copy(vv, val_hbm, out_v)
-    store_v.start()
     projection = scale * jnp.sum(fwd[...] * cv[...].astype(F32), axis=1, keepdims=True) / width
-    first = scale * inverse
-    second = inverse**3 * projection
-
-    def store_ig(j):
-        at = pl.ds(pl.multiple_of(j * 512, 512), 512)
-        return pltpu.make_async_copy(igv.at[:, at], ig_hbm.at[:, at], out_ig.at[j])
-
-    def finish(j):
-        at = pl.ds(pl.multiple_of(j * 512, 512), 512)
-        igv[:, at] = (first * back[:, at] - second * xv[:, at].astype(F32)).astype(BF16)
-        store_ig(j).start()
-
-    loop(0, width // 512, finish)
-    loop(n - EARLY, n, mix)
-
-    store_v.wait()
-    loop(0, width // 512, lambda j: store_ig(j).wait())
+    factors[0] = scale * inverse
+    factors[1] = inverse**3 * projection
+
     send_x(0, f1).wait_send()
     send_x(1, f3).wait_send()
     send_c.wait_send()
 
     def drain(k):
-        store_p(k).wait()
-        store_m(k).wait()
+        swap_p(k).wait_recv()
+        swap_m(k).wait_recv()
         gather_y(k).wait_send()
         gather_own(k).wait_send()
         gather_fwd(k).wait_send()
@@ -259,52 +232,96 @@
     loop(0, n, drain)
 
 
-def run(level, x, c, p, m):
+def place(values, xv, back, factors, pv, rp, mv, rm, vo, igo, po, mo, ig, new_p, new_m, done):
+    copies = []
+
+    def leave(source, target):
+        copy = pltpu.make_async_copy(source, target, done.at[len(copies)])
+        copy.start()
+        copies.append(copy)
+
+    leave(values, vo)
+    size = xv.shape[0] // PIECES
+    for j in range(PIECES):
+        at = pl.ds(j * size, size)
+        ig[at] = (factors[0, at] * back[at] - factors[1, at] * xv[at].astype(F32)).astype(BF16)
+        leave(ig.at[at], igo.at[at])
+    size = pv.shape[0] // PIECES
+    for j in range(PIECES):
+        at = pl.ds(j * size, size)
+        momentum = 0.5 * (mv[at] + rm[at].astype(F32))
+        new_m[at] = momentum
+        leave(new_m.at[at], mo.at[at])
+        new_p[at] = 0.5 * (pv[at] + rp[at].astype(F32)) - LEARN_RATE * momentum
+        leave(new_p.at[at], po.at[at])
+    for copy in copies:
+        copy.wait()
+
+
+def settle(*arrays):
+    values, xv, back, factors, pv, rp, mv, rm = arrays
+    results = (values, xv, pv, mv)
+    return pl.pallas_call(
+        place,
+        out_shape=tuple(jax.ShapeDtypeStruct(a.shape, a.dtype) for a in results),
+        in_specs=[pl.BlockSpec(memory_space=pltpu.VMEM)] * 8,
+        out_specs=(pl.BlockSpec(memory_space=pl.ANY),) * 4,
+        scratch_shapes=[
+            pltpu.VMEM(xv.shape, BF16),
+            pltpu.VMEM(pv.shape, F32),
+            pltpu.VMEM(mv.shape, F32),
+            pltpu.SemaphoreType.DMA((1 + 3 * PIECES,)),
+        ],
+        compiler_params=pltpu.CompilerParams(vmem_limit_bytes=28 * 2**20),
+        name="settle",
+    )(*arrays)
+
+
+def run(level, levels, x, c, p, m):
     tokens, width = x.shape
     rows, units = p.shape
     n = rows // CHUNK
+    relay = level == levels - 1
+    early = n // 2 if relay else n // 4
     dma = pltpu.SemaphoreType.DMA
-    anywhere = pl.BlockSpec(memory_space=pl.ANY)
     vmem = pltpu.VMEM
-    return pl.pallas_call(
-        functools.partial(kernel, 2**level),
+    shape = jax.ShapeDtypeStruct
+    outs = pl.pallas_call(
+        functools.partial(kernel, 2**level, early, relay),
         out_shape=(
-            jax.ShapeDtypeStruct((tokens, units), BF16),
-            jax.ShapeDtypeStruct((tokens, width), BF16),
-            jax.ShapeDtypeStruct((rows, units), F32),
-            jax.ShapeDtypeStruct((rows, units), F32),
+            shape((tokens, units), BF16),
+            shape((tokens, width), BF16),
+            shape((tokens, width), F32),
+            shape((2, tokens, 1), F32),
+            shape((rows, units), F32),
+            shape((rows, units), BF16),
+            shape((rows, units), F32),
+            shape((rows, units), BF16),
         ),
-        in_specs=[anywhere] * 4,
-        out_specs=(anywhere,) * 4,
+        in_specs=[pl.BlockSpec(memory_space=pl.ANY)] * 4,
+        out_specs=(pl.BlockSpec(memory_space=vmem),) * 8,
         scratch_shapes=[
-            vmem((tokens, width), BF16),
             vmem((2, tokens, rows), BF16),
             vmem((tokens, units), BF16),
             vmem((tokens, units), BF16),
             vmem((tokens, units), BF16),
-            vmem((rows, units), F32),
-            vmem((rows, units), F32),
             vmem((4, rows, units), BF16),
             vmem((rows, units), BF16),
             vmem((rows, units), BF16),
             vmem((rows, units), BF16),
-            vmem((rows, units), BF16),
-            vmem((rows, units), BF16),
             vmem((tokens, units), F32),
-            vmem((tokens, width), F32),
             vmem((tokens, 1), F32),
-            vmem((tokens, units), BF16),
-            vmem((tokens, width), BF16),
-            dma((n,)), dma, dma, dma, dma, dma((width // 512,)), dma((n,)), dma((n,)),
+            dma((n,)), dma, dma, dma,
             dma((2,)), dma((2,)), dma, dma,
             dma((n,)), dma((n,)), dma((n,)), dma((n,)), dma((n,)), dma((n,)),
             dma((n,)), dma((n,)), dma((n,)), dma((n,)), dma((n,)), dma((n,)),
         ],
         compiler_params=pltpu.CompilerParams(
-            collective_id=level, has_side_effects=True, vmem_limit_bytes=48 * 2**20
+            collective_id=level, has_side_effects=True, vmem_limit_bytes=30 * 2**20
         ),
         name="window" + str(level),
     )(x, c, p, m)
+    return settle(*outs)
 
 
 def on_device(inputs, cotangent, param, momentum, step):
@@ -312,7 +329,7 @@
     level = jnp.remainder(step, levels)
     outs = lax.switch(
         level,
-        [functools.partial(run, position) for position in range(levels)],
+        [functools.partial(run, position, levels) for position in range(levels)],
         inputs[0], cotangent[0], param[0], momentum[0],
     )
     return tuple(out[None] for out in outs)

time: 61.2 us -> 102 us (1.67)
  Pallas kernels: 54.9 us -> 99.7 us
  local copies, waits for them, and re-layouts: 4.66 us -> 0 us
    pallas_call x1 -> x2, Pallas kernels: 54.9 us -> 99.7 us  [the longest x1 96.3 us: run(): pl.pallas_call(functools.partial(kernel, 2 ** level, early, relay), out_s...]
    unnamed x4 -> x0, local copies, waits for them, and re-layouts: 4.66 us -> none
where the time goes in v2:
time: 102 us
  Pallas kernels  99.7 us (98%)
  between operations  1.51 us (1%)
    pallas_call x1, Pallas kernels, run(): pl.pallas_call(functools.partial(kernel, 2 ** level, early, relay), out_s...  96.3 us
    pallas_call x1, Pallas kernels, settle(): pl.pallas_call(place, out_shape=tuple((jax.ShapeDtypeStruct(a.shape, a.dt...  3.38 us

profile of v2, /device:TPU:1, one launch (start us, length us, event | category | flops | bytes accessed | tf_op | source)
XLA Modules:
  0.0 101.8 jit_solution(1122480468698167454)
XLA Ops:
  1.3 100.2 %conditional.1 = ((bf16[256,512]{1,0:T(8,128)(2,1)}, bf16[256,4096]{1,0:T(8,128)(2,1)}, f32[1024,512]{1,0:T(8,128)}, f32[1024,512]{1,0:T(8,128)})) conditional(s32[]{:T(128)} %clamp.3, (bf16[256,4096]{1,0:T(8,128)(2,1)}, bf16[256,512]{1,0:T(8,128)(2,1)}, f32[1024,512]{1,0:T(8,128)}, ...), branch_computations={%region_0.1_spmd.clone, %region_1.2_spmd.clone, %region_2.3_spmd.c... | conditional | bytes 8 | solution.py:330
  1.5 96.3 %window3.1 = (bf16[256,512]{1,0:T(8,128)(2,1)S(1)}, bf16[256,4096]{1,0:T(8,128)(2,1)S(1)}, f32[256,4096]{1,0:T(8,128)S(1)}, f32[2,256,1]{2,1,0:T(8,128)S(1)}, f3...) custom-call(bf16[256,4096]{1,0:T(8,128)(2,1)} %get-tuple-element.221, ...), custom_call_target="tpu_custom_call" | custom-call | tf_op jit(solution)/shard_map/cond/branch_3_fun/window3/pallas_call | solution.py:289
  97.8 3.4 %settle.9 = (bf16[256,512]{1,0:T(8,128)(2,1)}, bf16[256,4096]{1,0:T(8,128)(2,1)}, f32[1024,512]{1,0:T(8,128)}, f32[1024,512]{1,0:T(8,128)}) custom-call(bf16[256,512]{1,0:T(8,128)(2,1)S(1)} %get-tuple-element.225.values, bf16[256,4096]{1,0:T(8,128)(2,1)S(1)} %get-tuple-element.226.xv, f32[256,4096]{1,0:T(8,128)S(1)} %get-tuple-element.227.back, ...), custom_call_target="tpu_custom_call" | custom-call | tf_op jit(solution)/shard_map/cond/branch_3_fun/settle/pallas_call | solution.py:264

commit v3 on v2

--- a/solution.py
+++ b/solution.py
@@ -17,7 +17,7 @@
 BF16 = jnp.bfloat16
 
 CHUNK = 128
-PIECES = 4
+PIECES = 8
 
 
 def dot(a, b, ca, cb):
@@ -25,10 +25,10 @@
 
 
 def kernel(
-    stride, early, relay,
+    stride, early, depth, relay,
     x_hbm, c_hbm, p_hbm, m_hbm,
-    vv, xv, back, factors, pv, rp, mv, rm,
-    xs, cv, cs, css, w, gs, gr, ms, fwd, inv,
+    cv, xv, fwd, back, inv, pv, rp, mv, rm,
+    xs, cs, css, w, gs, gr, ms,
     in_p, in_x, in_c, in_m,
     xs_s, xs_r, cs_s, cs_r, ya_s, ya_r, so_s, so_r, sf_s, sf_r,
     g_s, g_r, ep_s, ep_r, em_s, em_r,
@@ -69,7 +69,7 @@
     load_m = pltpu.make_async_copy(m_hbm, mv, in_m)
 
     def send_x(j, owner):
-        return remote(x_hbm.at[:, block(owner)], xs.at[j], xs_s.at[j], xs_r.at[j], sib)
+        return remote(xv.at[:, block(owner)], xs.at[j], xs_s.at[j], xs_r.at[j], sib)
 
     send_c = remote(cs, css, cs_s, cs_r, sib)
 
@@ -110,32 +110,40 @@
     load_x.start()
     load_c.start()
     load_m.start()
-    pl.semaphore_wait(barrier, len(friends))
 
     def begin(k):
+        if not relay:
+            swap_p(k).start()
+
+    def shorten(k):
         load_p(k).wait()
         w[f, part(k)] = pv[part(k)].astype(BF16)
-        if not relay:
-            swap_p(k).start()
-
-        @pl.when(k < early)
-        def _():
-            gather_y(k).start()
-
-    loop(0, early, begin)
+
+    loop(0, early, shorten)
+    pl.semaphore_wait(barrier, len(friends))
+
+    def open_up(k):
+        begin(k)
+        gather_y(k).start()
+
+    def follow(k):
+        shorten(k)
+        begin(k)
+
+    loop(0, early, open_up)
+    loop(early, n, follow)
+    loop(0, n, lambda k: gather_own(k).start())
+
+    load_x.wait()
     send_x(1, f3).start()
     send_x(0, f1).start()
-    loop(early, n, begin)
-    loop(0, n, lambda k: gather_own(k).start())
-
-    load_x.wait()
     load_c.wait()
 
-    def square(j, total):
+    def add_square(j, total):
         part_x = xv[:, pl.ds(pl.multiple_of(j * 512, 512), 512)].astype(F32)
         return total + jnp.sum(part_x * part_x, axis=1, keepdims=True)
 
-    total = lax.fori_loop(0, width // 512, square, jnp.zeros((tokens, 1), F32))
+    total = lax.fori_loop(0, width // 512, add_square, jnp.zeros((tokens, 1), F32))
     inverse = lax.rsqrt(total / width + EPSILON)
     inv[...] = inverse
     cs[...] = (inverse * cv[...].astype(F32)).astype(BF16)
@@ -146,23 +154,9 @@
         theirs = dot(xs[j, :, part(k)], css[...], 0, 0)
         return scale * (mine + theirs)
 
-    send_x(1, f3).wait_recv()
-    send_c.wait_recv()
-
-    def give(k):
-        gs[part(k)] = term(f2, 1, k).astype(BF16)
-        send_g(k).start()
-
-    loop(0, n, give)
-
-    send_x(0, f1).wait_recv()
-    load_m.wait()
-
     def keep(k):
         at = part(k)
         mv[at] = MOMENTUM_BETA * mv[at] + WEIGHT_DECAY * pv[at] + term(f, 0, k)
-
-    loop(0, n, keep)
 
     def product(owner, k):
         piece = w[owner, part(k)]
@@ -186,10 +180,6 @@
         product(f2, k)
         gather_fwd(k).wait_recv()
         product(f3, k)
-
-    loop(0, early, pass_on)
-    loop(0, n, near)
-    loop(0, early, far)
 
     def fold(k):
         at = part(k)
@@ -199,40 +189,93 @@
         ms[at] = mid.astype(BF16)
         swap_m(k).start()
 
-    loop(0, n - 1, fold)
-    loop(early, n, lambda k: gather_y(k).start())
-    fold(n - 1)
-
-    def rest(k):
-        pass_on(k)
-        far(k)
-
-    loop(early, n, rest)
-
-    inverse = inv[...]
-    vv[...] = (scale * inverse * fwd[...]).astype(BF16)
-    projection = scale * jnp.sum(fwd[...] * cv[...].astype(F32), axis=1, keepdims=True) / width
-    factors[0] = scale * inverse
-    factors[1] = inverse**3 * projection
-
+    send_x(1, f3).wait_recv()
+    send_c.wait_recv()
+    send_x(0, f1).wait_recv()
+    load_m.wait()
+
+    def reduce_step(k):
+        gs[part(k)] = term(f2, 1, k).astype(BF16)
+
+        @pl.when(k < depth)
+        def _():
+            gather_y(early - depth + k).wait_send()
+
+        @pl.when(k >= depth)
+        def _():
+            send_g(k - depth).wait_send()
+
+        send_g(k).start()
+
+        @pl.when(k < early)
+        def _():
+            pass_on(k)
+
+        keep(k)
+        near(k)
+
+        @pl.when((k >= 1) & (k <= early))
+        def _():
+            far(k - 1)
+
+        @pl.when(k >= depth)
+        def _():
+            fold(k - depth)
+
+    loop(0, n, reduce_step)
+
+    def gather_step(k):
+        j = k - early
+
+        @pl.when(j < depth)
+        def _():
+            send_g(n - depth + j).wait_send()
+
+        @pl.when((j >= depth) & (k < n))
+        def _():
+            gather_y(k - depth).wait_send()
+
+        @pl.when(k < n)
+        def _():
+            gather_y(k).start()
+
+        @pl.when(j < depth)
+        def _():
+            fold(n - depth + j)
+
+        @pl.when((j >= 2) & (k < n + 2))
+        def _():
+            pass_on(k - 2)
+
+        @pl.when(j >= 3)
+        def _():
+            far(k - 3)
+
+    def drain_first(k):
+        gather_own(k).wait_send()
+        swap_p(k).wait_recv()
+        swap_p(k).wait_send()
+
+    def drain_last(k):
+        gather_fwd(k).wait_send()
+        swap_m(k).wait()
+
+    loop(early, n + 1, gather_step)
     send_x(0, f1).wait_send()
     send_x(1, f3).wait_send()
     send_c.wait_send()
-
-    def drain(k):
-        swap_p(k).wait_recv()
-        swap_m(k).wait_recv()
-        gather_y(k).wait_send()
-        gather_own(k).wait_send()
-        gather_fwd(k).wait_send()
-        send_g(k).wait_send()
-        swap_p(k).wait_send()
-        swap_m(k).wait_send()
-
-    loop(0, n, drain)
-
-
-def place(values, xv, back, factors, pv, rp, mv, rm, vo, igo, po, mo, ig, new_p, new_m, done):
+    if not relay:
+        loop(0, n, drain_first)
+    loop(n + 1, n + 3, gather_step)
+    if relay:
+        loop(0, n, drain_first)
+    loop(n - depth, n, lambda k: gather_y(k).wait_send())
+    loop(0, n, drain_last)
+
+
+def place(
+    cv, xv, fwd, back, inv, pv, rp, mv, rm, vo, igo, po, mo, values, ig, new_p, new_m, done
+):
     copies = []
 
     def leave(source, target):
@@ -240,12 +283,6 @@
         copy.start()
         copies.append(copy)
 
-    leave(values, vo)
-    size = xv.shape[0] // PIECES
-    for j in range(PIECES):
-        at = pl.ds(j * size, size)
-        ig[at] = (factors[0, at] * back[at] - factors[1, at] * xv[at].astype(F32)).astype(BF16)
-        leave(ig.at[at], igo.at[at])
     size = pv.shape[0] // PIECES
     for j in range(PIECES):
         at = pl.ds(j * size, size)
@@ -254,19 +291,34 @@
         leave(new_m.at[at], mo.at[at])
         new_p[at] = 0.5 * (pv[at] + rp[at].astype(F32)) - LEARN_RATE * momentum
         leave(new_p.at[at], po.at[at])
+    tokens, width = xv.shape
+    scale = width ** (-0.5)
+    inverse = inv[...]
+    values[...] = (scale * inverse * fwd[...]).astype(BF16)
+    leave(values, vo)
+    projection = scale * jnp.sum(fwd[...] * cv[...].astype(F32), axis=1, keepdims=True) / width
+    first = scale * inverse
+    second = inverse**3 * projection
+    size = tokens // PIECES
+    for j in range(PIECES):
+        at = pl.ds(j * size, size)
+        rows = slice(j * size, (j + 1) * size)
+        ig[at] = (first[rows] * back[at] - second[rows] * xv[at].astype(F32)).astype(BF16)
+        leave(ig.at[at], igo.at[at])
     for copy in copies:
         copy.wait()
 
 
 def settle(*arrays):
-    values, xv, back, factors, pv, rp, mv, rm = arrays
-    results = (values, xv, pv, mv)
+    cv, xv, fwd, back, inv, pv, rp, mv, rm = arrays
+    results = (cv, xv, pv, mv)
     return pl.pallas_call(
         place,
         out_shape=tuple(jax.ShapeDtypeStruct(a.shape, a.dtype) for a in results),
-        in_specs=[pl.BlockSpec(memory_space=pltpu.VMEM)] * 8,
+        in_specs=[pl.BlockSpec(memory_space=pltpu.VMEM)] * 9,
         out_specs=(pl.BlockSpec(memory_space=pl.ANY),) * 4,
         scratch_shapes=[
+            pltpu.VMEM(cv.shape, BF16),
             pltpu.VMEM(xv.shape, BF16),
             pltpu.VMEM(pv.shape, F32),
             pltpu.VMEM(mv.shape, F32),
@@ -282,35 +334,33 @@
     rows, units = p.shape
     n = rows // CHUNK
     relay = level == levels - 1
-    early = n // 2 if relay else n // 4
+    early, depth = (n // 2, n // 2) if relay else (n // 4, n // 4)
     dma = pltpu.SemaphoreType.DMA
     vmem = pltpu.VMEM
     shape = jax.ShapeDtypeStruct
     outs = pl.pallas_call(
-        functools.partial(kernel, 2**level, early, relay),
+        functools.partial(kernel, 2**level, early, depth, relay),
         out_shape=(
             shape((tokens, units), BF16),
             shape((tokens, width), BF16),
+            shape((tokens, units), F32),
             shape((tokens, width), F32),
-            shape((2, tokens, 1), F32),
+            shape((tokens, 1), F32),
             shape((rows, units), F32),
             shape((rows, units), BF16),
             shape((rows, units), F32),
             shape((rows, units), BF16),
         ),
         in_specs=[pl.BlockSpec(memory_space=pl.ANY)] * 4,
-        out_specs=(pl.BlockSpec(memory_space=vmem),) * 8,
+        out_specs=(pl.BlockSpec(memory_space=vmem),) * 9,
         scratch_shapes=[
             vmem((2, tokens, rows), BF16),
-            vmem((tokens, units), BF16),
             vmem((tokens, units), BF16),
             vmem((tokens, units), BF16),
             vmem((4, rows, units), BF16),
             vmem((rows, units), BF16),
             vmem((rows, units), BF16),
             vmem((rows, units), BF16),
-            vmem((tokens, units), F32),
-            vmem((tokens, 1), F32),
             dma((n,)), dma, dma, dma,
             dma((2,)), dma((2,)), dma, dma,
             dma((n,)), dma((n,)), dma((n,)), dma((n,)), dma((n,)), dma((n,)),

time: 102 us -> 57.6 us (0.56)
  Pallas kernels: 99.7 us -> 55.4 us
    pallas_call x1, Pallas kernels: 96.3 us -> 52.4 us  [run(): pl.pallas_call(functools.partial(kernel, 2 ** level, early, depth, relay)...]
where the time goes in v3:
time: 57.6 us; the launch traced here: 57.5 us
  Pallas kernels  55.4 us (96%)
  between operations  1.51 us (3%)
    pallas_call x1, Pallas kernels, run(): pl.pallas_call(functools.partial(kernel, 2 ** level, early, depth, relay)...  52.4 us
    pallas_call x1, Pallas kernels, settle(): pl.pallas_call(place, out_shape=tuple((jax.ShapeDtypeStruct(a.shape, a.dt...  3.09 us

profile of v3, /device:TPU:1, one launch (start us, length us, event | category | flops | bytes accessed | tf_op | source)
XLA Modules:
  0.0 57.5 jit_solution(1948829698277089768)
XLA Ops:
  1.3 56.0 %conditional.1 = ((bf16[256,512]{1,0:T(8,128)(2,1)}, bf16[256,4096]{1,0:T(8,128)(2,1)}, f32[1024,512]{1,0:T(8,128)}, f32[1024,512]{1,0:T(8,128)})) conditional(s32[]{:T(128)} %clamp.3, (bf16[256,4096]{1,0:T(8,128)(2,1)}, bf16[256,512]{1,0:T(8,128)(2,1)}, f32[1024,512]{1,0:T(8,128)}, ...), branch_computations={%region_0.1_spmd.clone, %region_1.2_spmd.clone, %region_2.3_spmd.c... | conditional | bytes 8 | solution.py:380
  1.3 52.4 %window0.1 = (bf16[256,512]{1,0:T(8,128)(2,1)S(1)}, bf16[256,4096]{1,0:T(8,128)(2,1)S(1)}, f32[256,512]{1,0:T(8,128)S(1)}, f32[256,4096]{1,0:T(8,128)S(1)}, f32[...) custom-call(bf16[256,4096]{1,0:T(8,128)(2,1)} %get-tuple-element.188, ...), custom_call_target="tpu_custom_call" | custom-call | tf_op jit(solution)/shard_map/cond/branch_0_fun/window0/pallas_call | solution.py:341
  53.7 3.1 %settle.6 = (bf16[256,512]{1,0:T(8,128)(2,1)}, bf16[256,4096]{1,0:T(8,128)(2,1)}, f32[1024,512]{1,0:T(8,128)}, f32[1024,512]{1,0:T(8,128)}) custom-call(bf16[256,512]{1,0:T(8,128)(2,1)S(1)} %get-tuple-element.192.cv, bf16[256,4096]{1,0:T(8,128)(2,1)S(1)} %get-tuple-element.193.xv, f32[256,512]{1,0:T(8,128)S(1)} %get-tuple-element.194.fwd, ...), custom_call_target="tpu_custom_call" | custom-call | tf_op jit(solution)/shard_map/cond/branch_0_fun/settle/pallas_call | solution.py:315
